TPU v7x, 32 devices: a whole 2x2x4 slice. The times are simulated.
32 devices in a mesh: scen: 4 (over y, x), intr: 8 (over z, core).
Axes of the slice: x: 2, y: 2, z: 4, core: 2. Of those that a mesh axis runs over, the one named last changes fastest.
Arguments:
- inverse_panels: bfloat16 [16, 2048, 2048], P('scen', 'intr'), may hold values from -0.125 to 0.125
- border_columns: bfloat16 [16, 2048, 512], P('scen', 'intr'), may hold values from -6 to 6
- border_tiles: bfloat16 [16, 16, 2048, 128], P('scen', None, 'intr'), may hold values from -0.125 to 0.125
- tile_rows: int32 [16, 16], P('scen'), may hold values from 0 to 31
- tile_slabs: int32 [16, 16], P('scen'), may hold values from 0 to 1
- tile_count: int32 [16], P('scen'), may hold values from 1 to 16
- base_slab: float32 [4096, 512], P(('scen', 'intr')), may hold values from -6 to 6
- earlier_panels: bfloat16 [8, 4096, 128], P(None, ('scen', 'intr')), may hold values from -0.25 to 0.25
- used_panels: int32 [4], replicated, may hold values from 0 to 7, as said below
Outputs:
- schur_slab: float32 [4096, 512], P(('scen', 'intr'))
Inputs may be any that keep to these rules, and one draw needn't show every extreme that they name: `used_panels`: distinct panel ids.
All inputs are finite; a program needn't handle non-finite values.
Results may differ from a plain program's by a relative error of at most 0.0026.
Values may be sent and summed in bfloat16 or wider, within the bound.
A program may use at most 128 MiB of HBM per device.

v0:
```python
import jax
import jax.numpy as jnp
from jax import lax
from jax.sharding import PartitionSpec as P

SLAB_ROWS = 4096
COLS = 512
SLAB_W = 256
TILE = 128
LIST = 16
NTILE = 32


def broadcast(value, axis, source):
    kept = jnp.where(lax.axis_index(axis) == source, value, 0).astype(value.dtype)
    return lax.psum(kept, axis)


def on_device(
    inverse_panels,
    border_columns,
    border_tiles,
    tile_rows,
    tile_slabs,
    tile_count,
    base_slab,
    earlier_panels,
    used_panels,
):
    scen_here = inverse_panels.shape[0]
    rows_here = inverse_panels.shape[1]
    nslab = COLS // SLAB_W
    gathered = lax.all_gather(border_columns, "intr", axis=1, tiled=True)
    applied = jnp.einsum(
        "srk,skc->src", inverse_panels, gathered, preferred_element_type=jnp.float32
    ).astype(jnp.bfloat16)
    split = applied.reshape(scen_here, rows_here, nslab, SLAB_W)
    scen_ids = jnp.arange(scen_here, dtype=jnp.int32)[:, None]
    chosen = split[scen_ids, :, tile_slabs]
    product = jnp.einsum(
        "slrt,slrw->sltw", border_tiles, chosen, preferred_element_type=jnp.float32
    )
    positions = jnp.arange(LIST, dtype=jnp.int32)
    live = (positions[None, :] < tile_count[:, None]).astype(jnp.float32)
    places = tile_rows * nslab + tile_slabs
    targets = jnp.arange(NTILE * nslab, dtype=jnp.int32)
    onehot = (places[:, :, None] == targets[None, None, :]).astype(jnp.float32) * live[:, :, None]
    onehot = onehot.reshape(scen_here * LIST, NTILE * nslab)
    total = jnp.dot(
        onehot.T, product.reshape(scen_here * LIST, TILE * SLAB_W), precision=lax.Precision.HIGHEST
    )
    partial_slab = (
        total.reshape(NTILE, nslab, TILE, SLAB_W).transpose(0, 2, 1, 3).reshape(SLAB_ROWS, COLS)
    )
    outer = lax.psum_scatter(partial_slab, "scen", scatter_dimension=0, tiled=True)
    coupling = lax.psum_scatter(outer, "intr", scatter_dimension=0, tiled=True)
    chosen_panels = earlier_panels[used_panels]
    rooted = broadcast(chosen_panels, "scen", 0)
    top_rows = lax.all_gather(rooted, "intr", axis=1, tiled=True)[:, :COLS, :]
    earlier = jnp.einsum("prt,pct->rc", chosen_panels, top_rows, preferred_element_type=jnp.float32)
    return base_slab - coupling - earlier


def solution(mesh):
    return jax.shard_map(
        on_device,
        mesh=mesh,
        in_specs=(
            P("scen", "intr", None),
            P("scen", "intr", None),
            P("scen", None, "intr", None),
            P("scen", None),
            P("scen", None),
            P("scen"),
            P(("scen", "intr"), None),
            P(None, ("scen", "intr"), None),
            P(),
        ),
        out_specs=P(("scen", "intr"), None),
        check_vma=False,
    )
```

profile of v0, /device:TPU:0, one launch (start us, length us, event | category | flops | bytes accessed | tf_op | source)
XLA Modules:
  0.0 289.8 jit_solution(16149499031638260580)
XLA Ops:
  7.4 0.0 copy-start
  7.4 0.0 all-gather.3.cloned.1.call-start
  7.4 0.7 all-gather.3.cloned.1.call-update
  8.1 0.0 all-reduce.2.cloned.1.call-start
  8.1 0.7 compare_select_fusion.1
  8.8 0.0 copy-done
  8.8 0.6 gather_fusion.1
  9.4 0.7 broadcast_select_fusion
  10.1 0.0 all-reduce.2.cloned.1.call-update
  10.1 0.0 reduce-scatter.3.cloned.1.call-start
  10.2 0.7 fusion.15
  10.9 0.7 multiply_add_fusion
  11.6 0.1 eq.35
  11.6 0.7 fusion.16
  12.4 0.1 reshape.67
  12.5 0.1 reshape.68
  12.5 82.1 %all-gather.3.cloned.1.call-done = bf16[4,2048,512]{2,1,0:T(8,128)(2,1)} async-done(((bf16[4,256,512]{2,1,0:T(8,128)(2,1)}), bf16[4,2048,512]{2,1,0:T(8,128)(2,1)}) %all-gather.3.cloned.1.call-update) | async-done | bytes 8388624 | tf_op jit(solution)/shard_map/all_gather | solution.py:33
  94.6 7.0 %convolution_convert_fusion = bf16[4,256,512]{2,1,0:T(8,128)(2,1)S(1)} fusion(bf16[4,256,2048]{2,1,0:T(8,128)(2,1)} %param.9, bf16[4,2048,512]{2,1,0:T(8,128)(2,1)} %all-gather.3.cloned.1.call-done), kind=kOutput, calls=%fused_computation.7 | convolution fusion | flops 2148007936 | bytes 13631488 | tf_op jit(solution)/shard_map/srk,skc->src/dot_general | solution.py:34
  101.6 0.1 copy.35
  101.7 5.8 %gather_fusion = bf16[64,256,256]{2,1,0:T(8,128)(2,1)} fusion(bf16[4,256,2,256]{3,1,2,0:T(8,128)(2,1)S(1)} %bitcast.51, s32[64]{0:T(128)S(1)} %reshape.68), kind=kCustom, calls=%fused_computation | custom fusion | bytes 16777728 | tf_op jit(solution)/shard_map/gather | solution.py:39
  107.5 10.2 %convolution_bitcast_fusion = f32[4,16,128,256]{2,3,1,0:T(8,128)} fusion(bf16[4,16,256,256]{3,2,1,0:T(8,128)(2,1)} %bitcast.52, bf16[4,16,256,128]{3,2,1,0:T(8,128)(2,1)} %param.11), kind=kOutput, calls=%fused_computation.5 | convolution fusion | flops 1073741824 | bytes 20971520 | tf_op jit(solution)/shard_map/slrt,slrw->sltw/dot_general | solution.py:40
  117.7 8.7 %copy.13 = f32[4,16,128,256]{3,2,1,0:T(8,128)} copy(f32[4,16,128,256]{2,3,1,0:T(8,128)} %convolution_bitcast_fusion) | data formatting | bytes 16777216 | tf_op jit(solution)/shard_map/slrt,slrw->sltw/dot_general | solution.py:40
  126.4 15.7 %fusion.2 = f32[32,128,2,256]{3,0,1,2:T(8,128)S(1)} fusion(f32[64]{0:T(128)S(1)} %reshape.67, s32[32,2]{0,1:T(2,128)S(1)} %multiply_add_fusion.1, s32[64]{0:T(128)S(1)} %eq.35, f32[8,8,128,256]{3,2,1,0:T(8,128)} %bitcast.54), kind=kOutput, calls=%fused_computation.6 | convolution fusion | flops 1610620928 | bytes 16777984 | tf_op jit(solution)/shard_map/dot_general | solution.py:49
  142.1 13.3 %copy.19 = f32[32,128,2,256]{3,2,1,0:T(2,128)S(1)} copy(f32[32,128,2,256]{3,0,1,2:T(8,128)S(1)} %fusion.2) | data formatting | bytes 16777216 | tf_op jit(solution)/shard_map/reshape | solution.py:53
  155.4 0.0 copy-start.1
  155.4 4.2 %copy.24 = f32[512,8,2,256]{3,1,2,0:T(8,128)} copy(f32[512,8,2,256]{3,2,1,0:T(2,128)S(1)} %bitcast.55) | data formatting | bytes 16777216
  159.6 0.0 copy-start.2
  159.6 0.0 reduce-scatter.3.cloned.1.call-update
  159.7 0.0 all-gather.5.cloned.1.call-start
  159.7 0.0 all-reduce.2.cloned.1.call-done
  159.7 0.7 all-gather.5.cloned.1.call-update
  160.4 0.0 reduce-scatter.5.cloned.1.call-start
  160.5 84.1 %reduce-scatter.3.cloned.1.call-done = f32[1024,512]{1,0:T(8,128)} async-done(((f32[4096,512]{1,0:T(8,128)}), f32[1024,512]{1,0:T(8,128)}) %reduce-scatter.3.cloned.1.call-update) | async-done | bytes 2097168 | tf_op jit(solution)/shard_map/reduce_scatter | solution.py:55
  244.6 0.0 reduce-scatter.5.cloned.1.call-update
  244.6 0.0 all-gather.5.cloned.1.call-done
  244.6 35.9 %reduce-scatter.5.cloned.1.call-done = f32[128,512]{1,0:T(8,128)} async-done(((f32[1024,512]{1,0:T(8,128)}), f32[128,512]{1,0:T(8,128)}) %reduce-scatter.5.cloned.1.call-update) | async-done | bytes 262160 | tf_op jit(solution)/shard_map/reduce_scatter | solution.py:56
  280.5 0.0 copy-done.2
  280.5 2.1 fusion.3
  282.6 0.0 copy-done.1
  (2 shorter events, 0.0 us)
Async XLA Ops:
  7.4 1.5 copy-start
  7.4 87.2 %all-gather.3.cloned.1.call-start = ((), (), s32[]{:S(2)}) async-start(), calls=%async_computation.2 | async-start | bytes 9437184 | tf_op jit(solution)/shard_map/all_gather | solution.py:33
  8.1 151.6 %all-reduce.2.cloned.1.call-start = ((), (), s32[]{:S(2)}) async-start(), calls=%async_computation.5 | async-start | bytes 262144 | tf_op jit(solution)/shard_map/psum | solution.py:16
  10.1 234.5 %reduce-scatter.3.cloned.1.call-start = ((), (), s32[]{:S(2)}) async-start(), calls=%async_computation.3 | async-start | bytes 10485760 | tf_op jit(solution)/shard_map/reduce_scatter | solution.py:55
  155.4 127.2 %copy-start.1 = (bf16[8,128,128]{2,1,0:T(8,128)(2,1)S(1)}, bf16[8,128,128]{2,1,0:T(8,128)(2,1)}, u32[]{:S(2)}) copy-start(bf16[8,128,128]{2,1,0:T(8,128)(2,1)} %param.16) | copy-start | bytes 786436
  159.6 120.9 %copy-start.2 = (f32[128,512]{1,0:T(8,128)S(1)}, f32[128,512]{1,0:T(8,128)}, u32[]{:S(2)}) copy-start(f32[128,512]{1,0:T(8,128)} %param.15) | copy-start | bytes 786436
  159.7 84.9 %all-gather.5.cloned.1.call-start = ((), (), s32[]{:S(2)}) async-start(), calls=%async_computation.6 | async-start | bytes 1179648 | tf_op jit(solution)/shard_map/all_gather | solution.py:59
  160.4 120.1 %reduce-scatter.5.cloned.1.call-start = ((), (), s32[]{:S(2)}) async-start(), calls=%async_computation.4 | async-start | bytes 2359296 | tf_op jit(solution)/shard_map/reduce_scatter | solution.py:56
Sparse Core Ops, SparseCore 0:
  9.8 84.7 all-gather.2
  162.2 20.6 all-gather.4
  244.7 35.7 reduce-scatter.4
Sparse Core Ops, SparseCore 1:
  11.4 44.3 all-reduce.1
  159.7 84.8 reduce-scatter.2
where the time goes:
time: 290 us
  waiting for transfers between devices  204 us (70%)
  matrix products  35 us (12%)
  local copies, waits for them, and re-layouts  32.9 us (11%)
  between operations  14.6 us (5%)
  other arithmetic  3.46 us (1%)
    reduce_scatter x1, waiting for transfers between devices, on_device(): lax.psum_scatter(partial_slab, 'scen', scatter_dimension=0, tiled=True)  84.1 us
    all_gather x1, waiting for transfers between devices, on_device(): gathered = lax.all_gather(border_columns, 'intr', axis=1, tiled=True)  82.1 us
    reduce_scatter x1, waiting for transfers between devices, on_device(): coupling = lax.psum_scatter(outer, 'intr', scatter_dimension=0, tiled=True)  35.9 us
    dot_general x1, matrix products, on_device(): jnp.dot(onehot.T, product.reshape(scen_here * LIST, TILE * SLAB_W), preci...  15.7 us
    reshape x1, local copies, waits for them, and re-layouts, on_device(): total.reshape(NTILE, nslab, TILE, SLAB_W).transpose(0, 2, 1, 3)  13.3 us
    dot_general x1, matrix products, on_device(): jnp.einsum('slrt,slrw->sltw', border_tiles, chosen, preferred_element_typ...  10.2 us
    dot_general x1, local copies, waits for them, and re-layouts, on_device(): jnp.einsum('slrt,slrw->sltw', border_tiles, chosen, preferred_element_typ...  8.68 us
    dot_general x1, matrix products, on_device(): jnp.einsum('srk,skc->src', inverse_panels, gathered, preferred_element_ty...  6.98 us
  transfers between devices with their start and end apart: 5, of which 3 were waited for; matrix products, arithmetic and copies ran while one was open for 24% of the time, Pallas kernels for 0%

commit v1 on v0

v1 whole, which is shorter than its diff:
```python
import functools

import jax
import jax.numpy as jnp
from jax import lax
from jax.experimental import pallas as pl
from jax.experimental.pallas import tpu as pltpu
from jax.sharding import PartitionSpec as P

SLAB_W = 256
TILE = 128
WIDTH = 128
MESH = pl.DeviceIdType.MESH
F32 = jnp.float32
BF16 = jnp.bfloat16


def kernel(
    groups,
    inner,
    used_ref,
    prev_ref,
    last_ref,
    inv_hbm,
    cols_hbm,
    tiles_hbm,
    base_hbm,
    panels_hbm,
    out_hbm,
    inv,
    gath,
    tiles,
    turned,
    base,
    panels,
    own_top,
    top,
    earlier,
    applied,
    chain,
    keep,
    pair_out,
    pair_in,
    mid,
    scen_out,
    scen_in,
    low,
    line_out,
    line_in,
    result,
    load_sem,
    own_sem,
    col_send,
    col_recv,
    hop_send,
    hop_recv,
    top_send,
    top_recv,
    pair_send,
    pair_recv,
    scen_send,
    scen_recv,
    line_send,
    line_recv,
    out_sem,
):
    scen_here, listed, rows, _ = tiles.shape
    mine_rows, cols = base.shape
    used = own_top.shape[0]
    chunks = cols // WIDTH
    zs = inner // 2
    sub = TILE // mine_rows
    nslab = cols // SLAB_W
    tops = cols // mine_rows
    me_s = lax.axis_index("scen")
    me_i = lax.axis_index("intr")
    z, c = me_i // 2, me_i % 2
    sibling = (me_s, z * 2 + 1 - c)

    def remote(src, dst, send, recv, device):
        return pltpu.make_async_remote_copy(
            src_ref=src, dst_ref=dst, send_sem=send, recv_sem=recv, device_id=device, device_id_type=MESH
        )

    loads = [
        pltpu.make_async_copy(src, dst, load_sem.at[n])
        for n, (src, dst) in enumerate(
            [(panels_hbm, panels), (tiles_hbm, tiles), (inv_hbm, inv), (base_hbm, base)]
        )
    ]
    for load in loads:
        load.start()

    barrier = pltpu.get_barrier_semaphore()
    partners = [(lax.rem(me_s + n, groups), me_i) for n in range(1, groups)]
    partners += [(me_s, lax.rem(z + n, zs) * 2 + c) for n in range(1, zs)]
    partners += [sibling]
    for partner in partners:
        pl.semaphore_signal(barrier, inc=1, device_id=partner, device_id_type=MESH)
    pl.semaphore_wait(barrier, len(partners))

    def slot(q, j):
        return gath.at[q, :, pl.ds(pl.multiple_of(j * rows, rows), rows), :]

    def own_block(q):
        return cols_hbm.at[:, :, pl.ds(q * WIDTH, WIDTH)]

    def col_copy(q, j, way, src):
        device = [(me_s, (z + 1) * 2 + c), (me_s, (z - 1) * 2 + c), sibling][way]
        return remote(src, slot(q, j), col_send.at[q, j, way], col_recv.at[q, j], device)

    def own_local(q):
        return pltpu.make_async_copy(own_block(q), slot(q, me_i), own_sem.at[q])

    def own_start(q):
        @pl.when(z < zs - 1)
        def _():
            col_copy(q, me_i, 0, own_block(q)).start()

        @pl.when(z > 0)
        def _():
            col_copy(q, me_i, 1, own_block(q)).start()

        col_copy(q, me_i, 2, own_block(q)).start()
        own_local(q).start()

    def top_slot(j):
        return top.at[:, pl.ds(pl.multiple_of(j * mine_rows, mine_rows), mine_rows), :]

    def top_copy(j, way):
        device = [(me_s, (z + 1) * 2 + c), (me_s, (z - 1) * 2 + c), sibling][way]
        return remote(top_slot(j), top_slot(j), top_send.at[j, way], top_recv.at[j], device)

    def pass_on(copy, d, has):
        @pl.when((z >= d) & has(z - d))
        def _():
            j = (z - d) * 2 + c
            copy(j, 0).wait_recv()

            @pl.when(z < zs - 1)
            def _():
                copy(j, 0).start()

            copy(j, 2).start()

        @pl.when((z + d < zs) & has(z + d))
        def _():
            j = (z + d) * 2 + c
            copy(j, 1).wait_recv()

            @pl.when(z > 0)
            def _():
                copy(j, 1).start()

            copy(j, 2).start()

    def relay(q, d):
        pass_on(lambda j, way: col_copy(q, j, way, slot(q, j)), d, lambda other: other >= 0)

    def has_top(other):
        return other < tops // 2

    def hop(n):
        return remote(
            own_top, top_slot(me_i), hop_send.at[n], hop_recv, (lax.rem(me_s + n, groups), me_i)
        )

    def top_local():
        return pltpu.make_async_copy(own_top, top_slot(me_i), load_sem.at[len(loads)])

    def pair_copy(q):
        return remote(pair_out.at[q], pair_in.at[q], pair_send.at[q], pair_recv.at[q], sibling)

    def scen_copy(q, n):
        return remote(
            scen_out.at[q, n - 1],
            scen_in.at[q, n - 1],
            scen_send.at[q, n - 1],
            scen_recv.at[q, n - 1],
            (lax.rem(me_s + n, groups), me_i),
        )

    def line_copy(q, n):
        return remote(
            line_out.at[q, n - 1],
            line_in.at[q, n - 1],
            line_send.at[q, n - 1],
            line_recv.at[q, n - 1],
            (me_s, lax.rem(z + n, zs) * 2 + c),
        )

    def compute(q):
        def apply(s, carry):
            applied[s] = jnp.dot(inv[s], gath[q, s], preferred_element_type=F32).astype(BF16)
            return carry

        lax.fori_loop(0, scen_here, apply, 0)
        batch = 4

        def multiply(s, carry):
            for n in range(listed // batch):
                product = jnp.dot(
                    turned[s, n * batch * TILE : (n + 1) * batch * TILE, :],
                    applied[s],
                    preferred_element_type=F32,
                )
                for m in range(batch):
                    e = s * listed + n * batch + m
                    block = product[m * TILE : (m + 1) * TILE].reshape(sub, mine_rows, WIDTH)
                    chain[e + 1] = block + chain[prev_ref[e]]
            return carry

        lax.fori_loop(0, scen_here, multiply, 0)
        slab = q * WIDTH // SLAB_W

        def place(k, carry):
            mine, other = 2 * k + c, 2 * k + 1 - c
            pair_out[q, k] = chain[last_ref[other // sub * nslab + slab], other % sub]
            keep[k] = chain[last_ref[mine // sub * nslab + slab], mine % sub]
            return carry

        lax.fori_loop(0, groups * zs, place, 0)
        pair_copy(q).start()

    def to_groups(q):
        pair_copy(q).wait_recv()
        for n in list(range(1, groups)) + [0]:
            at = pl.ds(lax.rem(me_s + n, groups) * zs, zs)
            block = keep[at] + pair_in[q, at]
            if n == 0:
                mid[q] = block
            else:
                scen_out[q, n - 1] = block.astype(BF16)
                scen_copy(q, n).start()

    def to_line(q):
        for n in range(1, groups):
            scen_copy(q, n).wait_recv()
        total = mid[q]
        for n in range(1, groups):
            total += scen_in[q, n - 1].astype(F32)
        low[q] = total
        for n in range(1, zs):
            line_out[q, n - 1] = low[q, lax.rem(z + n, zs)].astype(BF16)
            line_copy(q, n).start()

    def out_copy(q):
        at = pl.ds(q * WIDTH, WIDTH)
        return pltpu.make_async_copy(result.at[q], out_hbm.at[:, at], out_sem.at[q])

    def finish(q):
        at = slice(q * WIDTH, (q + 1) * WIDTH)
        total = low[q, z]
        for n in range(1, zs):
            line_copy(q, n).wait_recv()
            total += line_in[q, n - 1].astype(F32)
        result[q] = base[:, at] - total - earlier[:, at]
        out_copy(q).start()

    own_start(0)
    loads[0].wait()
    for p in range(used):
        own_top[p] = panels[used_ref[p]]

    @pl.when((me_s == 0) & (me_i < tops))
    def _():
        for n in range(1, groups):
            hop(n).start()
        top_local().start()

    loads[1].wait()

    def turn(s, carry):
        for n in range(listed):
            turned[s, n * TILE : (n + 1) * TILE, :] = tiles[s, n].T
        return carry

    lax.fori_loop(0, scen_here, turn, 0)
    chain[0] = jnp.zeros(chain.shape[1:], F32)
    loads[2].wait()
    loads[3].wait()

    for q in range(chunks):
        if q + 1 < chunks:
            own_start(q + 1)
        for d in range(1, zs):
            relay(q, d)
            if q > 0 and d == 1:
                to_line(q - 1)
        if q == 0:

            @pl.when(me_i < tops)
            def _():
                @pl.when(me_s == 0)
                def _():
                    top_local().wait()

                @pl.when(me_s > 0)
                def _():
                    hop(1).wait_recv()

                @pl.when(z < zs - 1)
                def _():
                    top_copy(me_i, 0).start()

                @pl.when(z > 0)
                def _():
                    top_copy(me_i, 1).start()

                top_copy(me_i, 2).start()

            for d in range(1, zs):
                pass_on(top_copy, d, has_top)
        else:
            finish(q - 1)
        own_local(q).wait()
        for other in range(zs):
            col_copy(q, other * 2 + 1 - c, 2, slot(q, other * 2 + 1 - c)).wait_recv()
        compute(q)
        if q == 0:
            for other in range(tops // 2):
                top_copy(other * 2 + 1 - c, 2).wait_recv()
            total = jnp.zeros((mine_rows, cols), F32)
            for p in range(used):
                total += lax.dot_general(
                    own_top[p], top[p], (((1,), (1,)), ((), ())), preferred_element_type=F32
                )
            earlier[...] = total
        to_groups(q)
    to_line(chunks - 1)
    finish(chunks - 1)

    def drain(copy, other):
        j = other * 2 + c

        @pl.when((z >= other) & (z < zs - 1))
        def _():
            copy(j, 0).wait_send()

        @pl.when((z <= other) & (z > 0))
        def _():
            copy(j, 1).wait_send()

        copy(j, 2).wait_send()

    def drain_chunk(q, carry):
        def one(other, inside):
            drain(lambda j, way: col_copy(q, j, way, slot(q, j)), other)
            return inside

        lax.fori_loop(0, zs, one, 0)
        pair_copy(q).wait_send()
        for n in range(1, groups):
            scen_copy(q, n).wait_send()
        for n in range(1, zs):
            line_copy(q, n).wait_send()
        return carry

    lax.fori_loop(0, chunks, drain_chunk, 0)
    for other in range(tops // 2):
        drain(top_copy, other)

    @pl.when((me_s == 0) & (me_i < tops))
    def _():
        for n in range(1, groups):
            hop(n).wait_send()

    for q in range(chunks):
        out_copy(q).wait()


def on_device(
    groups,
    inner,
    inverse_panels,
    border_columns,
    border_tiles,
    tile_rows,
    tile_slabs,
    tile_count,
    base_slab,
    earlier_panels,
    used_panels,
):
    scen_here, rows, depth = inverse_panels.shape
    cols = border_columns.shape[2]
    listed = border_tiles.shape[1]
    mine_rows = base_slab.shape[0]
    used = used_panels.shape[0]
    nslab = cols // SLAB_W
    chunks = cols // WIDTH
    zs = inner // 2
    sub = TILE // mine_rows
    tops = cols // mine_rows
    entries = scen_here * listed
    targets = mine_rows * groups * inner // TILE * nslab
    live = jnp.arange(listed, dtype=jnp.int32)[None, :] < tile_count[:, None]
    keys = jnp.where(live, tile_rows * nslab + tile_slabs, -1).reshape(entries)
    at = jnp.arange(entries, dtype=jnp.int32)
    same = (keys[None, :] == keys[:, None]) & (at[None, :] < at[:, None])
    prev = jnp.max(jnp.where(same, at[None, :] + 1, 0), axis=1)
    hits = keys[None, :] == jnp.arange(targets, dtype=jnp.int32)[:, None]
    last = jnp.max(jnp.where(hits, at[None, :] + 1, 0), axis=1)
    dma = pltpu.SemaphoreType.DMA
    smem = pl.BlockSpec(memory_space=pltpu.SMEM)
    anywhere = pl.BlockSpec(memory_space=pl.ANY)
    return pl.pallas_call(
        functools.partial(kernel, groups, inner),
        out_shape=jax.ShapeDtypeStruct((mine_rows, cols), F32),
        in_specs=[smem] * 3 + [anywhere] * 5,
        out_specs=anywhere,
        scratch_shapes=[
            pltpu.VMEM((scen_here, rows, depth), BF16),
            pltpu.VMEM((chunks, scen_here, depth, WIDTH), BF16),
            pltpu.VMEM(border_tiles.shape, BF16),
            pltpu.VMEM((scen_here, listed * TILE, rows), BF16),
            pltpu.VMEM((mine_rows, cols), F32),
            pltpu.VMEM(earlier_panels.shape, BF16),
            pltpu.VMEM((used, mine_rows, TILE), BF16),
            pltpu.VMEM((used, cols, TILE), BF16),
            pltpu.VMEM((mine_rows, cols), F32),
            pltpu.VMEM((scen_here, rows, WIDTH), BF16),
            pltpu.VMEM((entries + 1, sub, mine_rows, WIDTH), F32),
            pltpu.VMEM((groups * zs, mine_rows, WIDTH), F32),
            pltpu.VMEM((chunks, groups * zs, mine_rows, WIDTH), F32),
            pltpu.VMEM((chunks, groups * zs, mine_rows, WIDTH), F32),
            pltpu.VMEM((chunks, zs, mine_rows, WIDTH), F32),
            pltpu.VMEM((chunks, groups - 1, zs, mine_rows, WIDTH), BF16),
            pltpu.VMEM((chunks, groups - 1, zs, mine_rows, WIDTH), BF16),
            pltpu.VMEM((chunks, zs, mine_rows, WIDTH), F32),
            pltpu.VMEM((chunks, zs - 1, mine_rows, WIDTH), BF16),
            pltpu.VMEM((chunks, zs - 1, mine_rows, WIDTH), BF16),
            pltpu.VMEM((chunks, mine_rows, WIDTH), F32),
            dma((5,)),
            dma((chunks,)),
            dma((chunks, inner, 3)),
            dma((chunks, inner)),
            dma((groups,)),
            dma,
            dma((tops, 3)),
            dma((tops,)),
            dma((chunks,)),
            dma((chunks,)),
            dma((chunks, groups - 1)),
            dma((chunks, groups - 1)),
            dma((chunks, zs - 1)),
            dma((chunks, zs - 1)),
            dma((chunks,)),
        ],
        compiler_params=pltpu.CompilerParams(
            collective_id=0, has_side_effects=True, vmem_limit_bytes=60 * 1024 * 1024
        ),
        cost_estimate=pl.CostEstimate(
            flops=2 * scen_here * rows * cols * (depth + listed * TILE // nslab),
            bytes_accessed=2 * scen_here * rows * (depth + listed * TILE + cols),
            transcendentals=0,
        ),
    )(
        used_panels,
        prev,
        last,
        inverse_panels,
        border_columns,
        border_tiles,
        base_slab,
        earlier_panels,
    )


def solution(mesh):
    groups, inner = mesh.shape["scen"], mesh.shape["intr"]
    return jax.shard_map(
        functools.partial(on_device, groups, inner),
        mesh=mesh,
        in_specs=(
            P("scen", "intr", None),
            P("scen", "intr", None),
            P("scen", None, "intr", None),
            P("scen", None),
            P("scen", None),
            P("scen"),
            P(("scen", "intr"), None),
            P(None, ("scen", "intr"), None),
            P(),
        ),
        out_specs=P(("scen", "intr"), None),
        check_vma=False,
    )
```

time: 290 us -> 133 us (0.46)
  waiting for transfers between devices: 204 us -> 0 us
  Pallas kernels: 0 us -> 130 us
  matrix products: 35 us -> 0 us
  local copies, waits for them, and re-layouts: 32.9 us -> 1.76 us
  between operations: 14.6 us -> 0.01 us
    pallas_call x0 -> x1, Pallas kernels: none -> 130 us  [on_device(): pl.pallas_call(functools.partial(kernel, groups, inner), out_shape=jax.Sh...]
    reduce_scatter x2 -> x0, waiting for transfers between devices: 120 us -> none  [the longest x1 84.1 us: on_device(): lax.psum_scatter(partial_slab, 'scen', scatter_dimension=0, tiled=True)]
    all_gather x2 -> x0, waiting for transfers between devices: 82.1 us -> none  [the longest x1 82.1 us: on_device(): gathered = lax.all_gather(border_columns, 'intr', axis=1, tiled=True)]
    dot_general x4 -> x0, matrix products: 35 us -> none  [the longest x1 15.7 us: on_device(): jnp.dot(onehot.T, product.reshape(scen_here * LIST, TILE * SLAB_W), preci...]
    reshape x2 -> x0, local copies, waits for them, and re-layouts: 13.3 us -> none  [the longest x1 13.3 us: on_device(): total.reshape(NTILE, nslab, TILE, SLAB_W).transpose(0, 2, 1, 3)]
    dot_general x1 -> x0, local copies, waits for them, and re-layouts: 8.68 us -> none  [on_device(): jnp.einsum('slrt,slrw->sltw', border_tiles, chosen, preferred_element_typ...]
    gather x2 -> x0, local copies, waits for them, and re-layouts: 6.42 us -> none  [the longest x1 5.85 us: on_device(): chosen = split[scen_ids, :, tile_slabs]]
  transfers between devices with their start and end apart: 5 -> 0, of which waited for: 3 -> 0; matrix products, arithmetic and copies ran while one was open for 24% -> 0% of each run, Pallas kernels for 0% -> 0%
where the time goes in v1:
time: 133 us
  Pallas kernels  130 us (98%)
  local copies, waits for them, and re-layouts  1.76 us (1%)
  other arithmetic  1.53 us (1%)
    pallas_call x1, Pallas kernels, on_device(): pl.pallas_call(functools.partial(kernel, groups, inner), out_shape=jax.Sh...  130 us

profile of v1, /device:TPU:0, one launch (start us, length us, event | category | flops | bytes accessed | tf_op | source)
XLA Modules:
  0.0 133.2 jit_solution(15996064267648951602)
XLA Ops:
  0.0 0.8 add_select_fusion
  0.8 0.1 eq.10
  0.9 0.8 select_reduce_fusion
  1.6 129.9 %shard_map.91 = f32[128,512]{1,0:T(8,128)} custom-call(s32[4]{0:T(128)} %used_ref.1, s32[64]{0:T(128)} %get-tuple-element.6.prev_ref, s32[64]{0:T(128)} %get-tuple-element.5.last_ref, bf16[4,256,2048]{2,1,0:T(8,128)(2,1)} %inv_hbm.1, bf16[4,256,512]{2,1,0:T(8,128)(2,1)} %cols_hbm.1, bf16[4,16,256,128]{3,2,1,0:T(8,128)(2,1)} %tiles_hbm.1, ...), custom_call_target="tpu_custom_call" | custom-call | flops 3221225472 | bytes 9437184 | tf_op jit(solution)/shard_map/pallas_call | solution.py:407
  131.6 1.7 %copy.11 = f32[128,512]{1,0:T(8,128)} copy(f32[128,512]{1,0:T(8,128)} %shard_map.91) | data formatting | bytes 524288
  (1 shorter events, 0.0 us)

commit v2 on v1

--- a/solution.py
+++ b/solution.py
@@ -168,8 +168,11 @@
     def top_local():
         return pltpu.make_async_copy(own_top, top_slot(me_i), load_sem.at[len(loads)])
 
-    def pair_copy(q):
-        return remote(pair_out.at[q], pair_in.at[q], pair_send.at[q], pair_recv.at[q], sibling)
+    def pair_copy(q, n):
+        at = pl.ds(lax.rem(me_s + n, groups) * zs, zs)
+        return remote(
+            pair_out.at[q, at], pair_in.at[q, at], pair_send.at[q, n], pair_recv.at[q, n], sibling
+        )
 
     def scen_copy(q, n):
         return remote(
@@ -219,13 +222,15 @@
             keep[k] = chain[last_ref[mine // sub * nslab + slab], mine % sub]
             return carry
 
-        lax.fori_loop(0, groups * zs, place, 0)
-        pair_copy(q).start()
+        for n in list(range(1, groups)) + [0]:
+            first = lax.rem(me_s + n, groups) * zs
+            lax.fori_loop(first, first + zs, place, 0)
+            pair_copy(q, n).start()
 
     def to_groups(q):
-        pair_copy(q).wait_recv()
         for n in list(range(1, groups)) + [0]:
             at = pl.ds(lax.rem(me_s + n, groups) * zs, zs)
+            pair_copy(q, n).wait_recv()
             block = keep[at] + pair_in[q, at]
             if n == 0:
                 mid[q] = block
@@ -257,7 +262,9 @@
         result[q] = base[:, at] - total - earlier[:, at]
         out_copy(q).start()
 
+    top_hops = [[d for d in range(1, zs) if min(d, chunks - 2) == q] for q in range(chunks)]
     own_start(0)
+    own_start(1)
     loads[0].wait()
     for p in range(used):
         own_top[p] = panels[used_ref[p]]
@@ -281,12 +288,16 @@
     loads[3].wait()
 
     for q in range(chunks):
-        if q + 1 < chunks:
+        if 1 < q + 1 < chunks:
             own_start(q + 1)
         for d in range(1, zs):
             relay(q, d)
             if q > 0 and d == 1:
+                to_groups(q - 1)
+            if q > 0 and d == zs - 1:
                 to_line(q - 1)
+        for d in top_hops[q]:
+            pass_on(top_copy, d, has_top)
         if q == 0:
 
             @pl.when(me_i < tops)
@@ -309,15 +320,11 @@
 
                 top_copy(me_i, 2).start()
 
-            for d in range(1, zs):
-                pass_on(top_copy, d, has_top)
-        else:
-            finish(q - 1)
         own_local(q).wait()
         for other in range(zs):
             col_copy(q, other * 2 + 1 - c, 2, slot(q, other * 2 + 1 - c)).wait_recv()
         compute(q)
-        if q == 0:
+        if q == chunks - 2:
             for other in range(tops // 2):
                 top_copy(other * 2 + 1 - c, 2).wait_recv()
             total = jnp.zeros((mine_rows, cols), F32)
@@ -326,7 +333,10 @@
                     own_top[p], top[p], (((1,), (1,)), ((), ())), preferred_element_type=F32
                 )
             earlier[...] = total
-        to_groups(q)
+        if q > 1:
+            finish(q - 2)
+    finish(chunks - 2)
+    to_groups(chunks - 1)
     to_line(chunks - 1)
     finish(chunks - 1)
 
@@ -349,7 +359,8 @@
             return inside
 
         lax.fori_loop(0, zs, one, 0)
-        pair_copy(q).wait_send()
+        for n in range(groups):
+            pair_copy(q, n).wait_send()
         for n in range(1, groups):
             scen_copy(q, n).wait_send()
         for n in range(1, zs):
@@ -439,8 +450,8 @@
             dma,
             dma((tops, 3)),
             dma((tops,)),
-            dma((chunks,)),
-            dma((chunks,)),
+            dma((chunks, groups)),
+            dma((chunks, groups)),
             dma((chunks, groups - 1)),
             dma((chunks, groups - 1)),
             dma((chunks, zs - 1)),

time: 133 us -> 113 us (0.85)
  Pallas kernels: 130 us -> 110 us
    pallas_call x1, Pallas kernels: 130 us -> 110 us  [on_device(): pl.pallas_call(functools.partial(kernel, groups, inner), out_shape=jax.Sh...]
where the time goes in v2:
time: 113 us
  Pallas kernels  110 us (97%)
  local copies, waits for them, and re-layouts  1.76 us (2%)
  other arithmetic  1.53 us (1%)
    pallas_call x1, Pallas kernels, on_device(): pl.pallas_call(functools.partial(kernel, groups, inner), out_shape=jax.Sh...  110 us

profile of v2, /device:TPU:0, one launch (start us, length us, event | category | flops | bytes accessed | tf_op | source)
XLA Modules:
  0.0 112.9 jit_solution(7908164029534272400)
XLA Ops:
  0.0 0.8 add_select_fusion
  0.8 0.1 eq.10
  0.9 0.8 select_reduce_fusion
  1.6 109.6 %shard_map.91 = f32[128,512]{1,0:T(8,128)} custom-call(s32[4]{0:T(128)} %used_ref.1, s32[64]{0:T(128)} %get-tuple-element.6.prev_ref, s32[64]{0:T(128)} %get-tuple-element.5.last_ref, bf16[4,256,2048]{2,1,0:T(8,128)(2,1)} %inv_hbm.1, bf16[4,256,512]{2,1,0:T(8,128)(2,1)} %cols_hbm.1, bf16[4,16,256,128]{3,2,1,0:T(8,128)(2,1)} %tiles_hbm.1, ...), custom_call_target="tpu_custom_call" | custom-call | flops 3221225472 | bytes 9437184 | tf_op jit(solution)/shard_map/pallas_call | solution.py:418
  111.2 1.7 %copy.11 = f32[128,512]{1,0:T(8,128)} copy(f32[128,512]{1,0:T(8,128)} %shard_map.91) | data formatting | bytes 524288
  (1 shorter events, 0.0 us)
